TPU v7x, 128 devices: a whole 4x4x4 slice. The times are simulated.
128 devices in a mesh: ctx: 16 (over y, x), head: 8 (over z, core).
Axes of the slice: x: 4, y: 4, z: 4, core: 2. Of those that a mesh axis runs over, the one named last changes fastest.
Arguments:
- queries: bfloat16 [32768, 4096], P(('ctx', 'head')), may hold values from -26 to 26
- span_kv: bfloat16 [32768, 2048], P(('ctx', 'head')), may hold values from -6 to 6
- context_kv: bfloat16 [8, 262144, 256], P('head', 'ctx'), may hold values from -6 to 6
- selected: int32 [8, 64, 3], P('head'), may hold values from 0 to 511, as said below
Outputs:
- attended: bfloat16 [32768, 4096], P(('ctx', 'head'))
Inputs may be any that keep to these rules, and one draw needn't show every extreme that they name: `selected`: within one query block the 3 indices differ. For each key-value head and each run of 4 query blocks that one index of ctx holds, at most 2 of their selections lie in one range of 32 context blocks that one index of ctx holds, and exactly 2 in some range.
All inputs are finite; a program needn't handle non-finite values.
Results may differ from a plain program's by a relative error of at most 0.0057.
Values may be sent and summed in bfloat16 or wider, within the bound.
No kernel may reach another device: no remote copies, remote signals or barrier semaphores. Data moves between devices by JAX's collectives and lax.ppermute only.
A program may use at most 192 MiB of HBM per device.

v0:
```python
import jax
import jax.numpy as jnp
from jax import lax
from jax.sharding import PartitionSpec as P

BLK = 512
CAP = 2


def attend(query_tile, key_tile, value_tile, causal):
    row_count = query_tile.shape[0]
    head_width = key_tile.shape[1]
    group_heads = query_tile.shape[1] // head_width
    query_three = query_tile.reshape(row_count, group_heads, head_width)
    scores = jnp.einsum(
        "qgd,kd->gqk", query_three, key_tile, preferred_element_type=jnp.float32
    ) * head_width ** (-0.5)
    if causal:
        row_index = jnp.arange(row_count, dtype=jnp.int32)
        causal_keep = row_index[:, None] >= row_index[None, :]
        scores = jnp.where(causal_keep[None], scores, -jnp.inf)
    maximum = jnp.max(scores, axis=-1, keepdims=True)
    exponent = jnp.exp(scores - maximum)
    totals = jnp.sum(exponent, axis=-1, keepdims=True)
    weights = (exponent / totals).astype(jnp.bfloat16)
    mixed_out = jnp.einsum(
        "gqk,kd->qgd", weights, value_tile, preferred_element_type=jnp.float32
    ).astype(jnp.bfloat16)
    block_stat = maximum[..., 0] + jnp.log(totals[..., 0])
    return (mixed_out.reshape(row_count, group_heads * head_width), block_stat)


def combine(mixed_out, block_stats, head_width):
    blocks_q, count, group_heads, row_count = block_stats.shape
    peak_stat = jnp.max(block_stats, axis=1, keepdims=True)
    total_stat = peak_stat + jnp.log(
        jnp.sum(jnp.exp(block_stats - peak_stat), axis=1, keepdims=True)
    )
    factors = jnp.exp(block_stats - total_stat)
    values = mixed_out.astype(jnp.float32).reshape(
        blocks_q, count, row_count, group_heads, head_width
    )
    scaled = jnp.swapaxes(factors, 2, 3)[..., None] * values
    merged = jnp.sum(scaled, axis=1).astype(jnp.bfloat16)
    return merged.reshape(blocks_q * row_count, group_heads * head_width)


def local(queries, span_kv, context_kv, selected):
    local_queries, local_span = (
        lax.all_to_all(queries, "head", split_axis=1, concat_axis=0, tiled=True),
        lax.all_to_all(span_kv, "head", split_axis=1, concat_axis=0, tiled=True),
    )
    head_width = local_span.shape[1] // 2
    blocks_q = local_queries.shape[0] // BLK
    query_tiles = local_queries.reshape(blocks_q, BLK, local_queries.shape[1])
    own_tiles = local_span.reshape(blocks_q, BLK, 2 * head_width)
    stored_kv = context_kv[0]
    blocks_kv = stored_kv.shape[0] // BLK
    stored_tiles = stored_kv.reshape(blocks_kv, BLK, 2 * head_width)
    chosen = selected[0]
    topk_count = chosen.shape[1]
    ctx_ranks = lax.axis_size("ctx")
    my_rank = lax.axis_index("ctx")
    entries = blocks_q * topk_count
    flat_picks = chosen.reshape(ctx_ranks, entries)
    owners = flat_picks // blocks_kv
    within_block = flat_picks % blocks_kv
    entry_order = jnp.arange(entries, dtype=jnp.int32)
    earlier = entry_order[None, :] < entry_order[:, None]
    same_owner = owners[:, :, None] == owners[:, None, :]
    slot_index = jnp.sum((same_owner & earlier[None]).astype(jnp.int32), axis=-1)
    my_owners = lax.dynamic_index_in_dim(owners, my_rank, 0, keepdims=False)
    my_slots = lax.dynamic_index_in_dim(slot_index, my_rank, 0, keepdims=False)
    slot_lanes = jnp.arange(CAP, dtype=jnp.int32)
    served_mask = (owners == my_rank)[:, :, None] & (
        slot_index[:, :, None] == slot_lanes[None, None, :]
    )
    serve_block = jnp.sum(jnp.where(served_mask, within_block[:, :, None], 0), axis=1)
    pick_row = my_owners * CAP + my_slots
    outgoing = stored_tiles[serve_block]
    arrived = lax.all_to_all(outgoing, "ctx", split_axis=0, concat_axis=0, tiled=True)
    fetched = arrived.reshape(ctx_ranks * CAP, BLK, 2 * head_width)[pick_row]
    fetched = fetched.reshape(blocks_q, topk_count, BLK, 2 * head_width)

    def per_block(triple):
        query_tile, far_tiles, own_tile = triple
        far_out, far_stat = jax.vmap(
            lambda kv_tile: attend(
                query_tile, kv_tile[:, :head_width], kv_tile[:, head_width:], False
            )
        )(far_tiles)
        own_out, own_stat = attend(
            query_tile, own_tile[:, :head_width], own_tile[:, head_width:], True
        )
        return (
            jnp.concatenate([far_out, own_out[None]], axis=0),
            jnp.concatenate([far_stat, own_stat[None]], axis=0),
        )

    mixed_out, block_stats = lax.map(per_block, (query_tiles, fetched, own_tiles))
    merged = combine(mixed_out, block_stats, head_width)
    return lax.all_to_all(merged, "head", split_axis=0, concat_axis=1, tiled=True)


def solution(mesh):
    placed = (
        P(("ctx", "head"), None),
        P(("ctx", "head"), None),
        P("head", "ctx", None),
        P("head", None, None),
    )
    return jax.shard_map(
        local, mesh=mesh, in_specs=placed, out_specs=P(("ctx", "head"), None), check_vma=False
    )
```

profile of v0, /device:TPU:25, one launch (start us, length us, event | category | flops | bytes accessed | tf_op | source)
XLA Modules:
  0.0 289.5 jit_solution(8433969023011906187)
XLA Ops:
  0.0 4.1 %copy.95 = bf16[256,4096]{0,1:T(8,128)(2,1)} copy(bf16[256,4096]{1,0:T(8,128)(2,1)} %param.6) | data formatting | bytes 4194304 | tf_op args[0]
  4.1 6.0 %all-to-all-start.1 = ((bf16[256,8,512]{0,2,1:T(8,128)(2,1)}), bf16[256,8,512]{0,2,1:T(8,128)(2,1)S(1)}, u32[]{:S(2)}, u32[]{:S(2)}) async-start(bf16[256,8,512]{0,2,1:T(8,128)(2,1)} %bitcast.152), calls=%async_computation.1 | async-start | bytes 4194304 | tf_op jit(solution)/shard_map/all_to_all | solution.py:50
  11.0 8.3 %gather_fusion = bf16[32,512,256]{2,1,0:T(8,128)(2,1)} fusion(bf16[32,512,256]{2,1,0:T(8,128)(2,1)} %bitcast.156, s32[1024]{0:T(1024)S(1)} %pad_clamp_fusion.1), kind=kCustom, calls=%fused_computation | custom fusion | bytes 16777344 | tf_op jit(solution)/shard_map/gather | solution.py:80
  19.3 17.1 %all-to-all-done.1 = bf16[256,8,512]{0,2,1:T(8,128)(2,1)S(1)} async-done(((bf16[256,8,512]{0,2,1:T(8,128)(2,1)}), bf16[256,8,512]{0,2,1:T(8,128)(2,1)S(1)}, u32[]{:S(2)}, u32[]{:S(2)}) %all-to-all-start.1) | async-done | bytes 2097184 | tf_op jit(solution)/shard_map/all_to_all | solution.py:50
  36.4 6.7 %all-to-all-start = ((bf16[16,2,512,256]{3,2,1,0:T(8,128)(2,1)}), bf16[16,2,512,256]{3,2,1,0:T(8,128)(2,1)}, u32[]{:S(2)}, u32[]{:S(2)}) async-start(bf16[16,2,512,256]{3,2,1,0:T(8,128)(2,1)} %bitcast.147), calls=%async_computation | async-start | bytes 16777216 | tf_op jit(solution)/shard_map/all_to_all | solution.py:81
  44.2 121.3 %all-to-all-done = bf16[16,2,512,256]{3,2,1,0:T(8,128)(2,1)} async-done(((bf16[16,2,512,256]{3,2,1,0:T(8,128)(2,1)}), bf16[16,2,512,256]{3,2,1,0:T(8,128)(2,1)}, u32[]{:S(2)}, u32[]{:S(2)}) %all-to-all-start) | async-done | bytes 8388640 | tf_op jit(solution)/shard_map/all_to_all | solution.py:81
  165.5 5.5 %all-to-all-start.2 = ((bf16[256,8,256]{2,0,1:T(8,128)(2,1)}), bf16[256,8,256]{2,0,1:T(8,128)(2,1)S(1)}, u32[]{:S(2)}, u32[]{:S(2)}) async-start(bf16[256,8,256]{2,0,1:T(8,128)(2,1)} %bitcast.158), calls=%async_computation.2 | async-start | bytes 2097152 | tf_op jit(solution)/shard_map/all_to_all | solution.py:51
  171.1 2.4 copy.96
  173.5 5.9 %gather_fusion.1 = bf16[12,512,256]{2,1,0:T(8,128)(2,1)} fusion(bf16[32,512,256]{2,1,0:T(8,128)(2,1)} %bitcast.21, s32[1024]{0:T(1024)S(1)} %pad_clamp_fusion), kind=kCustom, calls=%fused_computation.1 | custom fusion | bytes 6291504 | tf_op jit(solution)/shard_map/gather | solution.py:82
  179.4 6.6 %all-to-all-done.2 = bf16[256,8,256]{2,0,1:T(8,128)(2,1)S(1)} async-done(((bf16[256,8,256]{2,0,1:T(8,128)(2,1)}), bf16[256,8,256]{2,0,1:T(8,128)(2,1)S(1)}, u32[]{:S(2)}, u32[]{:S(2)}) %all-to-all-start.2) | async-done | bytes 1048608 | tf_op jit(solution)/shard_map/all_to_all | solution.py:51
  186.1 57.2 %while.12 = (s32[]{:T(128)}, bf16[4,4,512,512]{2,3,1,0:T(8,128)(2,1)}, f32[4,4,4,512]{3,2,1,0:T(4,128)S(1)}, bf16[4,3,512,256]{3,2,1,0:T(8,128)(2,1)}, bf16[4,51...) while((s32[]{:T(128)}, bf16[4,4,512,512]{2,3,1,0:T(8,128)(2,1)}, ...), condition=%wide.region_7.8_spmd, body=%wide.region_2.7_spmd.sunk | while | flops 2193883136 | bytes 64290920 | solution.py:100
  193.7 2.1 fusion.36
  195.8 3.0 %fusion.37 = bf16[3,128,4,512]{3,1,2,0:T(8,128)(2,1)S(1)} fusion(f32[3,512,512,4]{2,1,3,0:T(8,128)S(1)} %get-tuple-element.131, f32[3,4,512]{2,1,0:T(4,128)S(1)} %fusion.36, f32[3,4,512]{2,1,0:T(4,128)S(1)} %get-tuple-element.132, bf16[3,512,256]{2,1,0:T(8,128)(2,1)S(1)} %dynamic-slice_bitcast_fusion.5), kind=kOutput, calls=%fused_computation.16.clone.1 | convolution fusion | flops 818675712 | bytes 14598144 | tf_op jit(solution)/shard_map/while/body/eval_jaxpr/vmap(gqk,kd->qgd)/dot_general | solution.py:26
  208.0 2.1 fusion.36
  210.1 3.0 %fusion.37 = bf16[3,128,4,512]{3,1,2,0:T(8,128)(2,1)S(1)} fusion(f32[3,512,512,4]{2,1,3,0:T(8,128)S(1)} %get-tuple-element.131, f32[3,4,512]{2,1,0:T(4,128)S(1)} %fusion.36, f32[3,4,512]{2,1,0:T(4,128)S(1)} %get-tuple-element.132, bf16[3,512,256]{2,1,0:T(8,128)(2,1)S(1)} %dynamic-slice_bitcast_fusion.5), kind=kOutput, calls=%fused_computation.16.clone.1 | convolution fusion | flops 818675712 | bytes 14598144 | tf_op jit(solution)/shard_map/while/body/eval_jaxpr/vmap(gqk,kd->qgd)/dot_general | solution.py:26
  222.3 2.1 fusion.36
  224.4 3.0 %fusion.37 = bf16[3,128,4,512]{3,1,2,0:T(8,128)(2,1)S(1)} fusion(f32[3,512,512,4]{2,1,3,0:T(8,128)S(1)} %get-tuple-element.131, f32[3,4,512]{2,1,0:T(4,128)S(1)} %fusion.36, f32[3,4,512]{2,1,0:T(4,128)S(1)} %get-tuple-element.132, bf16[3,512,256]{2,1,0:T(8,128)(2,1)S(1)} %dynamic-slice_bitcast_fusion.5), kind=kOutput, calls=%fused_computation.16.clone.1 | convolution fusion | flops 818675712 | bytes 14598144 | tf_op jit(solution)/shard_map/while/body/eval_jaxpr/vmap(gqk,kd->qgd)/dot_general | solution.py:26
  236.6 2.1 fusion.36
  238.7 3.0 %fusion.37 = bf16[3,128,4,512]{3,1,2,0:T(8,128)(2,1)S(1)} fusion(f32[3,512,512,4]{2,1,3,0:T(8,128)S(1)} %get-tuple-element.131, f32[3,4,512]{2,1,0:T(4,128)S(1)} %fusion.36, f32[3,4,512]{2,1,0:T(4,128)S(1)} %get-tuple-element.132, bf16[3,512,256]{2,1,0:T(8,128)(2,1)S(1)} %dynamic-slice_bitcast_fusion.5), kind=kOutput, calls=%fused_computation.16.clone.1 | convolution fusion | flops 818675712 | bytes 14598144 | tf_op jit(solution)/shard_map/while/body/eval_jaxpr/vmap(gqk,kd->qgd)/dot_general | solution.py:26
  243.4 7.1 %fusion.15 = bf16[4,512,512]{1,2,0:T(8,128)(2,1)} fusion(bf16[4,4,512,512]{2,3,1,0:T(8,128)(2,1)} %get-tuple-element.39, f32[4,4,512,4]{2,3,1,0:T(4,128)S(1)} %exponential_bitcast_fusion), kind=kLoop, calls=%fused_computation.36 | loop fusion | flops 11534336 | bytes 10616832 | tf_op jit(solution)/shard_map/reduce_sum | solution.py:44
  250.5 2.8 copy.99
  253.3 30.5 %all_to_all.53 = bf16[8,256,512]{2,1,0:T(8,128)(2,1)} all-to-all(bf16[8,256,512]{2,1,0:T(8,128)(2,1)S(1)} %bitcast.153), channel_id=1, replica_groups=mesh['ctx'=16,'head'=8] {'head'}, dimensions={0} | all-to-all | bytes 4194304 | tf_op jit(solution)/shard_map/all_to_all | solution.py:102
  283.8 2.8 copy.100
  286.7 2.9 copy.101
  (79 shorter events, 38.7 us)
Async XLA Ops:
  0.0 10.1 %copy-start.1 = (s32[1,64,3]{1,0,2:T(1,128)S(1)}, s32[1,64,3]{1,0,2:T(1,128)}, u32[]{:S(2)}) copy-start(s32[1,64,3]{1,0,2:T(1,128)} %param.9) | copy-start | bytes 2308
  4.1 32.3 %all-to-all-start.1 = ((bf16[256,8,512]{0,2,1:T(8,128)(2,1)}), bf16[256,8,512]{0,2,1:T(8,128)(2,1)S(1)}, u32[]{:S(2)}, u32[]{:S(2)}) async-start(bf16[256,8,512]{0,2,1:T(8,128)(2,1)} %bitcast.152), calls=%async_computation.1 | async-start | bytes 4194304 | tf_op jit(solution)/shard_map/all_to_all | solution.py:50
  36.4 6.7 %copy-start = (bf16[256,2048]{1,0:T(8,128)(2,1)S(1)}, bf16[256,2048]{1,0:T(8,128)(2,1)}, u32[]{:S(2)}) copy-start(bf16[256,2048]{1,0:T(8,128)(2,1)} %param.7) | copy-start | bytes 3145732
  36.4 129.1 %all-to-all-start = ((bf16[16,2,512,256]{3,2,1,0:T(8,128)(2,1)}), bf16[16,2,512,256]{3,2,1,0:T(8,128)(2,1)}, u32[]{:S(2)}, u32[]{:S(2)}) async-start(bf16[16,2,512,256]{3,2,1,0:T(8,128)(2,1)} %bitcast.147), calls=%async_computation | async-start | bytes 16777216 | tf_op jit(solution)/shard_map/all_to_all | solution.py:81
  165.5 20.6 %all-to-all-start.2 = ((bf16[256,8,256]{2,0,1:T(8,128)(2,1)}), bf16[256,8,256]{2,0,1:T(8,128)(2,1)S(1)}, u32[]{:S(2)}, u32[]{:S(2)}) async-start(bf16[256,8,256]{2,0,1:T(8,128)(2,1)} %bitcast.158), calls=%async_computation.2 | async-start | bytes 2097152 | tf_op jit(solution)/shard_map/all_to_all | solution.py:51
where the time goes:
time: 292 us; the launch traced here: 290 us
  waiting for transfers between devices  145 us (50%)
  local copies, waits for them, and re-layouts  40.8 us (14%)
  blocking collectives  30.5 us (10%)
  matrix products  28.4 us (10%)
  other arithmetic  26.3 us (9%)
  starting transfers between devices  18.2 us (6%)
    all_to_all x1, waiting for transfers between devices, local(): lax.all_to_all(outgoing, 'ctx', split_axis=0, concat_axis=0, tiled=True)  121 us
    all_to_all x1, blocking collectives, local(): lax.all_to_all(merged, 'head', split_axis=0, concat_axis=1, tiled=True)  30.5 us
    dot_general x8, matrix products, attend(): jnp.einsum('gqk,kd->qgd', weights, value_tile, preferred_element_type=jnp...  17.9 us
    all_to_all x1, waiting for transfers between devices, local(): lax.all_to_all(queries, 'head', split_axis=1, concat_axis=0, tiled=True)  17.1 us
    reduce_sum x8, other arithmetic, attend(): totals = jnp.sum(exponent, axis=-1, keepdims=True)  12.1 us
    dot_general x8, matrix products, attend(): jnp.einsum('qgd,kd->gqk', query_three, key_tile, preferred_element_type=j...  10.5 us
    gather x1, local copies, waits for them, and re-layouts, local(): outgoing = stored_tiles[serve_block]  8.29 us
    reduce_sum x1, other arithmetic, combine(): merged = jnp.sum(scaled, axis=1).astype(jnp.bfloat16)  7.09 us
  transfers between devices with their start and end apart: 3, of which 3 were waited for; matrix products, arithmetic and copies ran while one was open for 6% of the time, Pallas kernels for 0%

commit v1 on v0

v1 whole, which is shorter than its diff:
```python
import jax
import jax.numpy as jnp
import numpy as np
from jax import lax
from jax.experimental import pallas as pl
from jax.experimental.pallas import tpu as pltpu
from jax.sharding import PartitionSpec as P

BLK = 512
CAP = 2
DH = 128
GROUP = 4
TOPK = 3
QB = 4
ENTRIES = QB * TOPK
SIDE = 4
ONES = 16
C = DH ** -0.5 * 1.4426950408889634

ORDER = [
    (0, 1), (0, 3), (1, 0), (3, 0), (2, 2), (1, 1), (3, 3), (1, 3),
    (3, 1), (1, 2), (3, 2), (2, 1), (2, 3), (0, 2), (2, 0),
]
SELF = len(ORDER)
FIRST = 5
GROUPS = [[SELF] + list(range(0, 5)), list(range(5, 9)), list(range(9, 13))]
LAST = [13, 14]

VMEM = pl.BlockSpec(memory_space=pltpu.VMEM)
SMEM = pl.BlockSpec(memory_space=pltpu.SMEM)
ANY = pl.BlockSpec(memory_space=pl.ANY)
PARAMS = pltpu.CompilerParams(vmem_limit_bytes=32 * 1024 * 1024)


def place_table(members):
    table = np.full((SIDE * SIDE,), -1, np.int32)
    for place, number in enumerate(members):
        dy, dx = (0, 0) if number == SELF else ORDER[number]
        table[dy * SIDE + dx] = place
    return jnp.asarray(table)


def ctx_position():
    rank = lax.axis_index("ctx")
    return rank // SIDE, rank % SIDE


def serve_kernel(members, sel_ref, tiles_ref, *refs):
    outs, sem = refs[:-1], refs[-1]
    y, x = ctx_position()
    me = y * SIDE + x
    copies = []
    for out, number in zip(outs, members):
        dy, dx = (0, 0) if number == SELF else ORDER[number]
        asker = ((y + dy) % SIDE) * SIDE + (x + dx) % SIDE
        found = jnp.int32(0)
        which = [jnp.int32(0)] * CAP
        for e in range(ENTRIES):
            pick = sel_ref[asker * QB + e // TOPK, e % TOPK]
            hit = pick // 32 == me
            for s in range(CAP):
                which[s] = jnp.where(hit & (found == s), pick % 32, which[s])
            found = found + hit.astype(jnp.int32)
        for s in range(CAP):
            copy = pltpu.make_async_copy(tiles_ref.at[which[s]], out.at[s], sem.at[len(copies)])
            copy.start()
            copies.append(copy)
    for copy in copies:
        copy.wait()


def serve_call(members, sel, tiles):
    n = len(members)
    return pl.pallas_call(
        lambda *refs: serve_kernel(members, *refs),
        in_specs=[SMEM, ANY],
        out_specs=[VMEM] * n,
        out_shape=[jax.ShapeDtypeStruct((CAP, BLK, 2 * DH), tiles.dtype)] * n,
        scratch_shapes=[pltpu.SemaphoreType.DMA((CAP * n,))],
        compiler_params=PARAMS,
        name="serve",
    )(sel, tiles)


def pack_kernel(heads, q_ref, s_ref, out_ref, sem):
    width = GROUP * DH
    copies = []
    for h in range(heads):
        copies.append(
            pltpu.make_async_copy(
                q_ref.at[:, pl.ds(h * width, width)], out_ref.at[h, :, pl.ds(0, width)], sem.at[2 * h]
            )
        )
        copies.append(
            pltpu.make_async_copy(
                s_ref.at[:, pl.ds(h * 2 * DH, 2 * DH)], out_ref.at[h, :, pl.ds(width, 2 * DH)], sem.at[2 * h + 1]
            )
        )
    for copy in copies:
        copy.start()
    for copy in copies:
        copy.wait()


def pack_call(queries, span_kv, heads):
    rows = queries.shape[0]
    return pl.pallas_call(
        lambda *refs: pack_kernel(heads, *refs),
        in_specs=[ANY, ANY],
        out_specs=VMEM,
        out_shape=jax.ShapeDtypeStruct((heads, rows, (GROUP + 2) * DH), queries.dtype),
        scratch_shapes=[pltpu.SemaphoreType.DMA((2 * heads,))],
        compiler_params=PARAMS,
        name="pack",
    )(queries, span_kv)


def values_t(v):
    return jnp.concatenate([v.T, jnp.ones((ONES, BLK), v.dtype)], axis=0)


def scores_t(k, q):
    return lax.dot_general(k, q, (((1,), (1,)), ((), ())), preferred_element_type=jnp.float32)


def own_kernel(x_ref, acc, ml):
    def body(b, carry):
        k = x_ref[b, :, GROUP * DH:(GROUP + 1) * DH]
        vt = values_t(x_ref[b, :, (GROUP + 1) * DH:])
        key = lax.broadcasted_iota(jnp.int32, (BLK, BLK), 0)
        query = lax.broadcasted_iota(jnp.int32, (BLK, BLK), 1)
        found = [scores_t(k, x_ref[b, :, g * DH:(g + 1) * DH]) for g in range(GROUP)]
        for g in range(GROUP):
            s = jnp.where(key <= query, found[g], -jnp.inf)
            m = jnp.max(s, axis=0, keepdims=True)
            p = jnp.exp2((s - m) * C).astype(jnp.bfloat16)
            pv = jnp.dot(vt, p, preferred_element_type=jnp.float32)
            acc[b, g] = pv[:DH]
            ml[b, g, 0:1] = m
            ml[b, g, 1:2] = pv[DH:DH + 1]
        return carry

    lax.fori_loop(0, QB, body, 0)


def add_block(q, kv, acc, ml, at):
    k = kv[:, :DH]
    vt = values_t(kv[:, DH:])
    found = [scores_t(k, q[:, g * DH:(g + 1) * DH]) for g in range(GROUP)]
    for g in range(GROUP):
        s = found[g]
        m_old = ml[at, g, 0:1]
        m = jnp.maximum(m_old, jnp.max(s, axis=0, keepdims=True))
        p = jnp.exp2((s - m) * C).astype(jnp.bfloat16)
        alpha = jnp.exp2((m_old - m) * C)
        pv = jnp.dot(vt, p, preferred_element_type=jnp.float32)
        acc[at, g] = acc[at, g] * alpha + pv[:DH]
        ml[at, g, 0:1] = m
        ml[at, g, 1:2] = ml[at, g, 1:2] * alpha + pv[DH:DH + 1]


def each_arrived(sel_ref, place_ref, x_ref, kv_refs, q_s, kv_s, first, count, step):
    y, x = ctx_position()
    base = (y * SIDE + x) * QB

    def body(e, carry):
        pick = sel_ref[base + e // TOPK, e % TOPK]
        owner = pick // 32

        def earlier(f, n):
            same = sel_ref[base + f // TOPK, f % TOPK] // 32 == owner
            return n + same.astype(jnp.int32)

        slot = lax.fori_loop(0, e, earlier, jnp.int32(0))
        dy = (y - owner // SIDE + SIDE) % SIDE
        dx = (x - owner % SIDE + SIDE) % SIDE
        place = place_ref[dy * SIDE + dx]
        for i, ref in enumerate(kv_refs):
            @pl.when(place == i)
            def _(ref=ref):
                kv_s[...] = ref[slot]

        @pl.when(place >= 0)
        def _():
            q_s[...] = x_ref[e // TOPK, :, :GROUP * DH]
            step(e // TOPK)

        return carry

    lax.fori_loop(first, first + count, body, 0)


def far_kernel(n, sel_ref, place_ref, x_ref, *refs):
    kv_refs, (acc_in, ml_in, acc, ml, q_s, kv_s) = refs[:n], refs[n:]
    each_arrived(
        sel_ref, place_ref, x_ref, kv_refs, q_s, kv_s, 0, ENTRIES,
        lambda b: add_block(q_s, kv_s[...], acc, ml, b),
    )


def last_kernel(n, ahead, sel_ref, place_ref, x_ref, *refs):
    kv_refs, (acc_in, ml_in, same_ref, other_ref, acc, ml, q_s, kv_s, out_s) = refs[:n], refs[n:]
    rank = lax.axis_index("head")
    b = (rank // 2 + ahead) % QB
    core = rank % 2
    acc[0] = acc_in[b]
    ml[0] = ml_in[b]
    each_arrived(
        sel_ref, place_ref, x_ref, kv_refs, q_s, kv_s, b * TOPK, TOPK,
        lambda b: add_block(q_s, kv_s[...], acc, ml, 0),
    )
    for g in range(GROUP):
        out = acc[0, g] / ml[0, g, 1:2]
        out_s[:, g * DH:(g + 1) * DH] = out.T.astype(out_s.dtype)
    half = BLK // 2
    same_ref[...] = out_s[pl.ds(pl.multiple_of(core * half, half), half), :]
    other_ref[...] = out_s[pl.ds(pl.multiple_of((1 - core) * half, half), half), :]


ACC = (QB, GROUP, DH, BLK)
ML = (QB, GROUP, 8, BLK)


def state_shapes():
    return [jax.ShapeDtypeStruct(ACC, jnp.float32), jax.ShapeDtypeStruct(ML, jnp.float32)]


def cost(blocks):
    units = int(blocks * GROUP)
    return pl.CostEstimate(
        flops=units * 4 * BLK * BLK * DH, bytes_accessed=units * BLK * DH * 2, transcendentals=units * BLK * BLK
    )


def own_call(x):
    return pl.pallas_call(
        own_kernel,
        in_specs=[VMEM],
        out_specs=[VMEM, VMEM],
        out_shape=state_shapes(),
        compiler_params=PARAMS,
        cost_estimate=cost(QB),
        name="own_blocks",
    )(x)


def far_call(sel, place, x, tiles, acc, ml):
    n = len(tiles)
    return pl.pallas_call(
        lambda *refs: far_kernel(n, *refs),
        in_specs=[SMEM, SMEM] + [VMEM] * (n + 3),
        out_specs=[VMEM, VMEM],
        out_shape=state_shapes(),
        scratch_shapes=[pltpu.VMEM((BLK, GROUP * DH), x.dtype), pltpu.VMEM((BLK, 2 * DH), x.dtype)],
        input_output_aliases={n + 3: 0, n + 4: 1},
        compiler_params=PARAMS,
        cost_estimate=cost(n * 0.75),
        name="far_blocks",
    )(sel, place, x, *tiles, acc, ml)


def last_call(ahead, sel, place, x, tiles, acc, ml):
    n = len(tiles)
    half = BLK // 2
    return pl.pallas_call(
        lambda *refs: last_kernel(n, ahead, *refs),
        in_specs=[SMEM, SMEM] + [VMEM] * (n + 3),
        out_specs=[VMEM, VMEM],
        out_shape=[jax.ShapeDtypeStruct((half, GROUP * DH), x.dtype)] * 2,
        scratch_shapes=[
            pltpu.VMEM((1,) + ACC[1:], jnp.float32),
            pltpu.VMEM((1,) + ML[1:], jnp.float32),
            pltpu.VMEM((BLK, GROUP * DH), x.dtype),
            pltpu.VMEM((BLK, 2 * DH), x.dtype),
            pltpu.VMEM((BLK, GROUP * DH), x.dtype),
        ],
        compiler_params=PARAMS,
        cost_estimate=cost(1),
        name="last_blocks",
    )(sel, place, x, *tiles, acc, ml)


def assemble_kernel(steps, *refs):
    pieces, out_ref = refs[:-1], refs[-1]
    rank = lax.axis_index("head")
    z, core = rank // 2, rank % 2
    width = GROUP * DH
    for (dz, dc), piece in zip(steps, pieces):
        sender = ((z - dz + QB) % QB) * 2 + (core + dc) % 2
        out_ref[:, pl.ds(pl.multiple_of(sender * width, width), width)] = piece[...]


def assemble_call(steps, pieces, heads):
    rows, width = pieces[0].shape
    return pl.pallas_call(
        lambda *refs: assemble_kernel(steps, *refs),
        in_specs=[VMEM] * len(pieces),
        out_specs=VMEM,
        out_shape=jax.ShapeDtypeStruct((rows, heads * width), pieces[0].dtype),
        compiler_params=PARAMS,
        name="assemble",
    )(*pieces)


def ctx_shift(value, dy, dx):
    pairs = [
        (y * SIDE + x, ((y + dy) % SIDE) * SIDE + (x + dx) % SIDE) for y in range(SIDE) for x in range(SIDE)
    ]
    return lax.ppermute(value, "ctx", pairs)


def head_shift(value, dz, dc):
    pairs = [(z * 2 + c, ((z + dz) % QB) * 2 + (c + dc) % 2) for z in range(QB) for c in range(2)]
    return lax.ppermute(value, "head", pairs)


def local(queries, span_kv, context_kv, selected):
    heads = lax.axis_size("head")
    rows = queries.shape[0]
    sel = selected[0]
    stored = context_kv[0]
    tiles = stored.reshape(stored.shape[0] // BLK, BLK, 2 * DH)

    numbers = list(range(SELF + 1))
    sent = dict(zip(numbers[:FIRST], serve_call(numbers[:FIRST], sel, tiles)))
    sent.update(zip(numbers[FIRST:], serve_call(numbers[FIRST:], sel, tiles)))
    packed = pack_call(queries, span_kv, heads)

    arrived = {SELF: sent[SELF]}
    for number, (dy, dx) in enumerate(ORDER):
        arrived[number] = ctx_shift(sent[number], dy, dx)
    x = lax.all_to_all(packed, "head", split_axis=0, concat_axis=0, tiled=True)
    x = x.reshape(QB, heads * rows // QB, (GROUP + 2) * DH)

    acc, ml = own_call(x)
    for members in GROUPS:
        acc, ml = far_call(sel, place_table(members), x, [arrived[i] for i in members], acc, ml)

    steps, pieces = [], []
    for dz in (2, 1, 3, 0):
        same, other = last_call(dz, sel, place_table(LAST), x, [arrived[i] for i in LAST], acc, ml)
        for dc, piece in ((0, same), (1, other)):
            steps.append((dz, dc))
            pieces.append(head_shift(piece, dz, dc) if dz or dc else piece)
    return assemble_call(steps, pieces, heads)


def solution(mesh):
    placed = (
        P(("ctx", "head"), None),
        P(("ctx", "head"), None),
        P("head", "ctx", None),
        P("head", None, None),
    )
    return jax.shard_map(
        local, mesh=mesh, in_specs=placed, out_specs=P(("ctx", "head"), None), check_vma=False
    )
```

time: 292 us -> 186 us (0.64)
  waiting for transfers between devices: 145 us -> 32.5 us
  starting transfers between devices: 18.2 us -> 83.7 us
  Pallas kernels: 0 us -> 50.4 us
  blocking collectives: 30.5 us -> 0 us
  matrix products: 28.4 us -> 0 us
  other arithmetic: 26.3 us -> 0 us
  local copies, waits for them, and re-layouts: 40.8 us -> 16.1 us
    all_to_all x3 -> x1, waiting for transfers between devices: 145 us -> 0.01 us  [local(): x = lax.all_to_all(packed, 'head', split_axis=0, concat_axis=0, tiled=True)]
    ppermute x0 -> x22, starting transfers between devices: none -> 77.6 us  [the longest x15 61.7 us: ctx_shift(): return lax.ppermute(value, 'ctx', pairs)]
    pallas_call x0 -> x12, Pallas kernels: none -> 50.4 us  [the longest x3 28.6 us: far_call(): pl.pallas_call(lambda *refs: far_kernel(n, *refs), in_specs=[SMEM, SMEM]...]
    ppermute x0 -> x22, waiting for transfers between devices: none -> 32.5 us  [the longest x15 24.6 us: ctx_shift(): return lax.ppermute(value, 'ctx', pairs)]
    all_to_all x1 -> x0, blocking collectives: 30.5 us -> none  [local(): lax.all_to_all(merged, 'head', split_axis=0, concat_axis=1, tiled=True)]
    dot_general x16 -> x0, matrix products: 28.4 us -> none  [the longest x8 17.9 us: attend(): jnp.einsum('gqk,kd->qgd', weights, value_tile, preferred_element_type=jnp...]
    reduce_sum x12 -> x0, other arithmetic: 19.6 us -> none  [the longest x8 12.1 us: attend(): totals = jnp.sum(exponent, axis=-1, keepdims=True)]
    gather x2 -> x0, local copies, waits for them, and re-layouts: 14.2 us -> none  [the longest x1 8.29 us: local(): outgoing = stored_tiles[serve_block]]
  transfers between devices with their start and end apart: 3 -> 23, of which waited for: 3 -> 6; matrix products, arithmetic and copies ran while one was open for 6% -> 0% of each run, Pallas kernels for 0% -> 25%
where the time goes in v1:
time: 186 us; the launch traced here: 183 us
  starting transfers between devices  83.7 us (45%)
  Pallas kernels  50.4 us (27%)
  waiting for transfers between devices  32.5 us (17%)
  local copies, waits for them, and re-layouts  16.1 us (9%)
    ppermute x15, starting transfers between devices, ctx_shift(): return lax.ppermute(value, 'ctx', pairs)  61.7 us
    pallas_call x3, Pallas kernels, far_call(): pl.pallas_call(lambda *refs: far_kernel(n, *refs), in_specs=[SMEM, SMEM]...  28.6 us
    ppermute x15, waiting for transfers between devices, ctx_shift(): return lax.ppermute(value, 'ctx', pairs)  24.6 us
    unnamed x63, local copies, waits for them, and re-layouts  16.1 us
    ppermute x7, starting transfers between devices, head_shift(): return lax.ppermute(value, 'head', pairs)  15.9 us
    pallas_call x4, Pallas kernels, last_call(): pl.pallas_call(lambda *refs: last_kernel(n, ahead, *refs), in_specs=[SMEM...  8.53 us
    ppermute x7, waiting for transfers between devices, head_shift(): return lax.ppermute(value, 'head', pairs)  7.88 us
    pallas_call x2, Pallas kernels, serve_call(): pl.pallas_call(lambda *refs: serve_kernel(members, *refs), in_specs=[SMEM...  6.95 us
  transfers between devices with their start and end apart: 23, of which 6 were waited for; matrix products, arithmetic and copies ran while one was open for 0% of the time, Pallas kernels for 25%

profile of v1, /device:TPU:25, one launch (start us, length us, event | category | flops | bytes accessed | tf_op | source)
XLA Modules:
  0.0 183.1 jit_solution(4781692614343609379)
XLA Ops:
  4.9 6.1 %all-to-all-start = ((bf16[8,256,768]{2,1,0:T(8,128)(2,1)}), bf16[8,256,768]{2,1,0:T(8,128)(2,1)S(1)}, u32[]{:S(2)}, u32[]{:S(2)}) async-start(bf16[8,256,768]{2,1,0:T(8,128)(2,1)} %copy-done.1), calls=%async_computation | async-start | bytes 6291456 | tf_op jit(solution)/shard_map/all_to_all | solution.py:332
  11.2 3.4 %copy-done = bf16[1,16384,256]{2,1,0:T(8,128)(2,1)S(1)} copy-done((bf16[1,16384,256]{2,1,0:T(8,128)(2,1)S(1)}, bf16[1,16384,256]{2,1,0:T(8,128)(2,1)}, u32[]{:S(2)}) %copy-start) | copy-done | bytes 8388632
  14.5 4.0 %serve.2 = (bf16[2,512,256]{2,1,0:T(8,128)(2,1)S(1)}, bf16[2,512,256]{2,1,0:T(8,128)(2,1)S(1)}, bf16[2,512,256]{2,1,0:T(8,128)(2,1)S(1)}, bf16[2,512,256]{2,1,0:...) custom-call(s32[64,3]{1,0:T(8,128)S(1)} %bitcast.13, ...), custom_call_target="tpu_custom_call" | custom-call | tf_op jit(solution)/shard_map/serve/pallas_call | solution.py:74
  20.2 2.4 %collective-permute-start.2 = (bf16[2,512,256]{2,1,0:T(8,128)(2,1)S(1)}, bf16[2,512,256]{2,1,0:T(8,128)(2,1)S(1)}, u32[]{:S(2)}, u32[]{:S(2)}) collective-permute-start(bf16[2,512,256]{2,1,0:T(8,128)(2,1)S(1)} %get-tuple-element.39), channel_id=1, source_target_pairs={{0,48},{8,56},{16,32},{24,40},{32,80},{40,88},{48,64},{56,72},{64,... | collective-permute-start | bytes 1572872 | tf_op jit(solution)/shard_map/ppermute | solution.py:309
  24.0 2.3 %collective-permute-start.7 = (bf16[2,512,256]{2,1,0:T(8,128)(2,1)S(1)}, bf16[2,512,256]{2,1,0:T(8,128)(2,1)S(1)}, u32[]{:S(2)}, u32[]{:S(2)}) collective-permute-start(bf16[2,512,256]{2,1,0:T(8,128)(2,1)S(1)} %get-tuple-element.44), channel_id=1, source_target_pairs={{0,120},{8,96},{16,104},{24,112},{32,24},{40,0},{48,8},{56,16},{64... | collective-permute-start | bytes 1572872 | tf_op jit(solution)/shard_map/ppermute | solution.py:309
  28.6 2.9 %serve.3 = (bf16[2,512,256]{2,1,0:T(8,128)(2,1)S(1)}, bf16[2,512,256]{2,1,0:T(8,128)(2,1)S(1)}, bf16[2,512,256]{2,1,0:T(8,128)(2,1)S(1)}, bf16[2,512,256]{2,1,0:T(8,128)(2,1)}, bf16[2,512,256]{2,1,0:T(8,128)(2,1)}) custom-call(s32[64,3]{1,0:T(8,128)S(1)} %bitcast.14, bf16[32,512,256]{2,1,0:T(8,128)(2,1)S(1)} %bitcast.12), custom_call_target="tpu_custom_call" | custom-call | tf_op jit(solution)/shard_map/serve/pallas_call | solution.py:74
  31.5 4.7 %collective-permute-done.2.refs_3_ = bf16[2,512,256]{2,1,0:T(8,128)(2,1)S(1)} collective-permute-done((bf16[2,512,256]{2,1,0:T(8,128)(2,1)S(1)}, bf16[2,512,256]{2,1,0:T(8,128)(2,1)S(1)}, u32[]{:S(2)}, u32[]{:S(2)}) %collective-permute-start.2) | collective-permute-done | bytes 524320 | tf_op jit(solution)/shard_map/ppermute | solution.py:309
  38.2 9.5 %collective-permute-done.6.refs_3_ = bf16[2,512,256]{2,1,0:T(8,128)(2,1)S(1)} collective-permute-done((bf16[2,512,256]{2,1,0:T(8,128)(2,1)S(1)}, bf16[2,512,256]{2,1,0:T(8,128)(2,1)S(1)}, u32[]{:S(2)}, u32[]{:S(2)}) %collective-permute-start.6) | collective-permute-done | bytes 524320 | tf_op jit(solution)/shard_map/ppermute | solution.py:309
  52.8 6.0 %collective-permute-done.8.refs_5_ = bf16[2,512,256]{2,1,0:T(8,128)(2,1)S(1)} collective-permute-done((bf16[2,512,256]{2,1,0:T(8,128)(2,1)S(1)}, bf16[2,512,256]{2,1,0:T(8,128)(2,1)S(1)}, u32[]{:S(2)}, u32[]{:S(2)}) %collective-permute-start.8) | collective-permute-done | bytes 524320 | tf_op jit(solution)/shard_map/ppermute | solution.py:309
  60.9 3.9 %collective-permute-start.14 = (bf16[2,512,256]{2,1,0:T(8,128)(2,1)}, bf16[2,512,256]{2,1,0:T(8,128)(2,1)}, u32[]{:S(2)}, u32[]{:S(2)}) collective-permute-start(bf16[2,512,256]{2,1,0:T(8,128)(2,1)} %get-tuple-element.52), channel_id=1, source_target_pairs={{0,80},{8,88},{16,64},{24,72},{32,112},{40,120},{48,96},{56,104},{... | collective-permute-start | bytes 1572872 | tf_op jit(solution)/shard_map/ppermute | solution.py:309
  64.9 4.4 %collective-permute-done.10.refs_4_ = bf16[2,512,256]{2,1,0:T(8,128)(2,1)S(1)} collective-permute-done((bf16[2,512,256]{2,1,0:T(8,128)(2,1)S(1)}, bf16[2,512,256]{2,1,0:T(8,128)(2,1)S(1)}, u32[]{:S(2)}, u32[]{:S(2)}) %collective-permute-start.10) | collective-permute-done | bytes 524320 | tf_op jit(solution)/shard_map/ppermute | solution.py:309
  70.1 2.6 %collective-permute-start.3 = (bf16[2,512,256]{2,1,0:T(8,128)(2,1)}, bf16[2,512,256]{2,1,0:T(8,128)(2,1)}, u32[]{:S(2)}, u32[]{:S(2)}) collective-permute-start(bf16[2,512,256]{2,1,0:T(8,128)(2,1)} %get-tuple-element.40), channel_id=1, source_target_pairs={{0,112},{8,120},{16,96},{24,104},{32,16},{40,24},{48,0},{56,8},{64... | collective-permute-start | bytes 1572872 | tf_op jit(solution)/shard_map/ppermute | solution.py:309
  76.2 3.2 %collective-permute-start.5 = (bf16[2,512,256]{2,1,0:T(8,128)(2,1)}, bf16[2,512,256]{2,1,0:T(8,128)(2,1)}, u32[]{:S(2)}, u32[]{:S(2)}) collective-permute-start(bf16[2,512,256]{2,1,0:T(8,128)(2,1)} %get-tuple-element.42), channel_id=1, source_target_pairs={{0,88},{8,64},{16,72},{24,80},{32,120},{40,96},{48,104},{56,112},{... | collective-permute-start | bytes 1572872 | tf_op jit(solution)/shard_map/ppermute | solution.py:309
  79.4 4.3 %own_blocks.1 = (f32[4,4,128,512]{3,2,1,0:T(8,128)S(1)}, f32[4,4,8,512]{3,2,1,0:T(8,128)S(1)}) custom-call(bf16[4,512,768]{2,1,0:T(8,128)(2,1)S(1)} %bitcast.3), custom_call_target="tpu_custom_call" | custom-call | flops 2147483648 | bytes 2097152 | tf_op jit(solution)/shard_map/own_blocks/pallas_call | solution.py:236
  83.8 36.3 %collective-permute-start = (bf16[2,512,256]{2,1,0:T(8,128)(2,1)S(1)}, bf16[2,512,256]{2,1,0:T(8,128)(2,1)S(1)}, u32[]{:S(2)}, u32[]{:S(2)}) collective-permute-start(bf16[2,512,256]{2,1,0:T(8,128)(2,1)S(1)} %copy-done.29), channel_id=1, source_target_pairs={{0,16},{8,24},{16,0},{24,8},{32,48},{40,56},{48,32},{56,40},{64,80... | collective-permute-start | bytes 1572872 | tf_op jit(solution)/shard_map/ppermute | solution.py:309
  120.5 14.0 %far_blocks.3 = (f32[4,4,128,512]{3,2,1,0:T(8,128)S(1)}, f32[4,4,8,512]{3,2,1,0:T(8,128)S(1)}) custom-call(s32[64,3]{1,0:T(8,128)S(1)} %bitcast.15, s32[16]{0:T(128)S(1)} %copy-done.25, bf16[4,512,768]{2,1,0:T(8,128)(2,1)S(1)} %bitcast.4, bf16[2,512,256]{2,1,0:T(8,128)(2,1)S(1)} %copy-done.15, ...), custom_call_target="tpu_custom_call", output_to_operand_aliasing={{0}: (9, {}), {1}: (10, {})} | custom-call | flops 2415919104 | bytes 2359296 | tf_op jit(solution)/shard_map/far_blocks/pallas_call | solution.py:249
  134.6 5.0 %far_blocks.4 = (f32[4,4,128,512]{3,2,1,0:T(8,128)S(1)}, f32[4,4,8,512]{3,2,1,0:T(8,128)S(1)}) custom-call(s32[64,3]{1,0:T(8,128)S(1)} %bitcast.16, s32[16]{0:T(128)S(1)} %copy-done.24, bf16[4,512,768]{2,1,0:T(8,128)(2,1)S(1)} %bitcast.5, bf16[2,512,256]{2,1,0:T(8,128)(2,1)S(1)} %copy-done.7, ...), custom_call_target="tpu_custom_call", output_to_operand_aliasing={{0}: (7, {}), {1}: (8, {})} | custom-call | flops 1610612736 | bytes 1572864 | tf_op jit(solution)/shard_map/far_blocks/pallas_call | solution.py:249
  139.7 9.6 %far_blocks.5 = (f32[4,4,128,512]{3,2,1,0:T(8,128)S(1)}, f32[4,4,8,512]{3,2,1,0:T(8,128)S(1)}) custom-call(s32[64,3]{1,0:T(8,128)S(1)} %bitcast.17, s32[16]{0:T(128)S(1)} %copy-done.23, bf16[4,512,768]{2,1,0:T(8,128)(2,1)S(1)} %bitcast.6, bf16[2,512,256]{2,1,0:T(8,128)(2,1)S(1)} %copy-done.5, ...), custom_call_target="tpu_custom_call", output_to_operand_aliasing={{0}: (7, {}), {1}: (8, {})} | custom-call | flops 1610612736 | bytes 1572864 | tf_op jit(solution)/shard_map/far_blocks/pallas_call | solution.py:249
  151.6 6.5 %collective-permute-start.16 = (bf16[256,512]{1,0:T(8,128)(2,1)S(1)}, bf16[256,512]{1,0:T(8,128)(2,1)S(1)}, u32[]{:S(2)}, u32[]{:S(2)}) collective-permute-start(bf16[256,512]{1,0:T(8,128)(2,1)S(1)} %get-tuple-element.62), channel_id=1, source_target_pairs={{0,5},{1,4},{2,7},{3,6},{4,1},{5,0},{6,3},{7,2},{8,13},{9,12},{10,... | collective-permute-start | bytes 786440 | tf_op jit(solution)/shard_map/ppermute | solution.py:314
  162.3 3.2 %collective-permute-start.18 = (bf16[256,512]{1,0:T(8,128)(2,1)S(1)}, bf16[256,512]{1,0:T(8,128)(2,1)S(1)}, u32[]{:S(2)}, u32[]{:S(2)}) collective-permute-start(bf16[256,512]{1,0:T(8,128)(2,1)S(1)} %get-tuple-element.64), channel_id=1, source_target_pairs={{0,3},{1,2},{2,5},{3,4},{4,7},{5,6},{6,1},{7,0},{8,11},{9,10},{10,... | collective-permute-start | bytes 786440 | tf_op jit(solution)/shard_map/ppermute | solution.py:314
  165.5 2.4 %last_blocks.6 = (bf16[256,512]{1,0:T(8,128)(2,1)S(1)}, bf16[256,512]{1,0:T(8,128)(2,1)S(1)}) custom-call(s32[64,3]{1,0:T(8,128)S(1)} %bitcast.20, s32[16]{0:T(128)S(1)} %copy-done.22, bf16[4,512,768]{2,1,0:T(8,128)(2,1)S(1)} %bitcast.9, bf16[2,512,256]{2,1,0:T(8,128)(2,1)S(1)} %collective-permute-done.refs_3_, ...), custom_call_target="tpu_custom_call" | custom-call | flops 536870912 | bytes 524288 | tf_op jit(solution)/shard_map/last_blocks/pallas_call | solution.py:265
  167.9 2.7 %collective-permute-start.19 = (bf16[256,512]{1,0:T(8,128)(2,1)S(1)}, bf16[256,512]{1,0:T(8,128)(2,1)S(1)}, u32[]{:S(2)}, u32[]{:S(2)}) collective-permute-start(bf16[256,512]{1,0:T(8,128)(2,1)S(1)} %get-tuple-element.65), channel_id=1, source_target_pairs={{0,6},{1,7},{2,0},{3,1},{4,2},{5,3},{6,4},{7,5},{8,14},{9,15},{10,... | collective-permute-start | bytes 786440 | tf_op jit(solution)/shard_map/ppermute | solution.py:314
  173.8 5.4 %collective-permute-done.18.refs_3_ = bf16[256,512]{1,0:T(8,128)(2,1)S(1)} collective-permute-done((bf16[256,512]{1,0:T(8,128)(2,1)S(1)}, bf16[256,512]{1,0:T(8,128)(2,1)S(1)}, u32[]{:S(2)}, u32[]{:S(2)}) %collective-permute-start.18) | collective-permute-done | bytes 262176 | tf_op jit(solution)/shard_map/ppermute | solution.py:314
  179.2 2.5 %collective-permute-done.20.refs_5_ = bf16[256,512]{1,0:T(8,128)(2,1)S(1)} collective-permute-done((bf16[256,512]{1,0:T(8,128)(2,1)S(1)}, bf16[256,512]{1,0:T(8,128)(2,1)S(1)}, u32[]{:S(2)}, u32[]{:S(2)}) %collective-permute-start.20) | collective-permute-done | bytes 262176 | tf_op jit(solution)/shard_map/ppermute | solution.py:314
  (97 shorter events, 35.4 us)
Async XLA Ops:
  4.9 74.4 %all-to-all-start = ((bf16[8,256,768]{2,1,0:T(8,128)(2,1)}), bf16[8,256,768]{2,1,0:T(8,128)(2,1)S(1)}, u32[]{:S(2)}, u32[]{:S(2)}) async-start(bf16[8,256,768]{2,1,0:T(8,128)(2,1)} %copy-done.1), calls=%async_computation | async-start | bytes 6291456 | tf_op jit(solution)/shard_map/all_to_all | solution.py:332
  20.2 16.0 %collective-permute-start.2 = (bf16[2,512,256]{2,1,0:T(8,128)(2,1)S(1)}, bf16[2,512,256]{2,1,0:T(8,128)(2,1)S(1)}, u32[]{:S(2)}, u32[]{:S(2)}) collective-permute-start(bf16[2,512,256]{2,1,0:T(8,128)(2,1)S(1)} %get-tuple-element.39), channel_id=1, source_target_pairs={{0,48},{8,56},{16,32},{24,40},{32,80},{40,88},{48,64},{56,72},{64,... | collective-permute-start | bytes 1572872 | tf_op jit(solution)/shard_map/ppermute | solution.py:309
  22.6 25.1 %collective-permute-start.6 = (bf16[2,512,256]{2,1,0:T(8,128)(2,1)S(1)}, bf16[2,512,256]{2,1,0:T(8,128)(2,1)S(1)}, u32[]{:S(2)}, u32[]{:S(2)}) collective-permute-start(bf16[2,512,256]{2,1,0:T(8,128)(2,1)S(1)} %get-tuple-element.43), channel_id=1, source_target_pairs={{0,40},{8,48},{16,56},{24,32},{32,72},{40,80},{48,88},{56,64},{64,... | collective-permute-start | bytes 1572872 | tf_op jit(solution)/shard_map/ppermute | solution.py:309
  24.0 26.8 %collective-permute-start.7 = (bf16[2,512,256]{2,1,0:T(8,128)(2,1)S(1)}, bf16[2,512,256]{2,1,0:T(8,128)(2,1)S(1)}, u32[]{:S(2)}, u32[]{:S(2)}) collective-permute-start(bf16[2,512,256]{2,1,0:T(8,128)(2,1)S(1)} %get-tuple-element.44), channel_id=1, source_target_pairs={{0,120},{8,96},{16,104},{24,112},{32,24},{40,0},{48,8},{56,16},{64... | collective-permute-start | bytes 1572872 | tf_op jit(solution)/shard_map/ppermute | solution.py:309
  26.2 32.6 %collective-permute-start.8 = (bf16[2,512,256]{2,1,0:T(8,128)(2,1)S(1)}, bf16[2,512,256]{2,1,0:T(8,128)(2,1)S(1)}, u32[]{:S(2)}, u32[]{:S(2)}) collective-permute-start(bf16[2,512,256]{2,1,0:T(8,128)(2,1)S(1)} %get-tuple-element.45), channel_id=1, source_target_pairs={{0,56},{8,32},{16,40},{24,48},{32,88},{40,64},{48,72},{56,80},{64,... | collective-permute-start | bytes 1572872 | tf_op jit(solution)/shard_map/ppermute | solution.py:309
  28.1 32.0 %collective-permute-start.9 = (bf16[2,512,256]{2,1,0:T(8,128)(2,1)S(1)}, bf16[2,512,256]{2,1,0:T(8,128)(2,1)S(1)}, u32[]{:S(2)}, u32[]{:S(2)}) collective-permute-start(bf16[2,512,256]{2,1,0:T(8,128)(2,1)S(1)} %get-tuple-element.46), channel_id=1, source_target_pairs={{0,104},{8,112},{16,120},{24,96},{32,8},{40,16},{48,24},{56,0},{64... | collective-permute-start | bytes 1572872 | tf_op jit(solution)/shard_map/ppermute | solution.py:309
  31.5 88.9 %copy-start.25 = (s32[16]{0:T(128)S(1)}, s32[16]{0:T(128)}, u32[]{:S(2)}) copy-start(s32[16]{0:T(128)} %constant.8.clone.refs_1_) | copy-start | bytes 196
  37.0 32.3 %collective-permute-start.10 = (bf16[2,512,256]{2,1,0:T(8,128)(2,1)S(1)}, bf16[2,512,256]{2,1,0:T(8,128)(2,1)S(1)}, u32[]{:S(2)}, u32[]{:S(2)}) collective-permute-start(bf16[2,512,256]{2,1,0:T(8,128)(2,1)S(1)} %get-tuple-element.48), channel_id=1, source_target_pairs={{0,8},{8,16},{16,24},{24,0},{32,40},{40,48},{48,56},{56,32},{64,72... | collective-permute-start | bytes 1572872 | tf_op jit(solution)/shard_map/ppermute | solution.py:309
  48.5 24.2 %collective-permute-start.11 = (bf16[2,512,256]{2,1,0:T(8,128)(2,1)S(1)}, bf16[2,512,256]{2,1,0:T(8,128)(2,1)S(1)}, u32[]{:S(2)}, u32[]{:S(2)}) collective-permute-start(bf16[2,512,256]{2,1,0:T(8,128)(2,1)S(1)} %get-tuple-element.49), channel_id=1, source_target_pairs={{0,24},{8,0},{16,8},{24,16},{32,56},{40,32},{48,40},{56,48},{64,88... | collective-permute-start | bytes 1572872 | tf_op jit(solution)/shard_map/ppermute | solution.py:309
  51.6 23.8 %collective-permute-start.12 = (bf16[2,512,256]{2,1,0:T(8,128)(2,1)S(1)}, bf16[2,512,256]{2,1,0:T(8,128)(2,1)S(1)}, u32[]{:S(2)}, u32[]{:S(2)}) collective-permute-start(bf16[2,512,256]{2,1,0:T(8,128)(2,1)S(1)} %get-tuple-element.50), channel_id=1, source_target_pairs={{0,32},{8,40},{16,48},{24,56},{32,64},{40,72},{48,80},{56,88},{64,... | collective-permute-start | bytes 1572872 | tf_op jit(solution)/shard_map/ppermute | solution.py:309
  59.6 24.2 %collective-permute-start.13 = (bf16[2,512,256]{2,1,0:T(8,128)(2,1)}, bf16[2,512,256]{2,1,0:T(8,128)(2,1)}, u32[]{:S(2)}, u32[]{:S(2)}) collective-permute-start(bf16[2,512,256]{2,1,0:T(8,128)(2,1)} %get-tuple-element.51), channel_id=1, source_target_pairs={{0,96},{8,104},{16,112},{24,120},{32,0},{40,8},{48,16},{56,24},{64... | collective-permute-start | bytes 1572872 | tf_op jit(solution)/shard_map/ppermute | solution.py:309
  60.9 59.1 %collective-permute-start.14 = (bf16[2,512,256]{2,1,0:T(8,128)(2,1)}, bf16[2,512,256]{2,1,0:T(8,128)(2,1)}, u32[]{:S(2)}, u32[]{:S(2)}) collective-permute-start(bf16[2,512,256]{2,1,0:T(8,128)(2,1)} %get-tuple-element.52), channel_id=1, source_target_pairs={{0,80},{8,88},{16,64},{24,72},{32,112},{40,120},{48,96},{56,104},{... | collective-permute-start | bytes 1572872 | tf_op jit(solution)/shard_map/ppermute | solution.py:309
  70.1 69.5 %collective-permute-start.3 = (bf16[2,512,256]{2,1,0:T(8,128)(2,1)}, bf16[2,512,256]{2,1,0:T(8,128)(2,1)}, u32[]{:S(2)}, u32[]{:S(2)}) collective-permute-start(bf16[2,512,256]{2,1,0:T(8,128)(2,1)} %get-tuple-element.40), channel_id=1, source_target_pairs={{0,112},{8,120},{16,96},{24,104},{32,16},{40,24},{48,0},{56,8},{64... | collective-permute-start | bytes 1572872 | tf_op jit(solution)/shard_map/ppermute | solution.py:309
  73.5 66.1 %collective-permute-start.4 = (bf16[2,512,256]{2,1,0:T(8,128)(2,1)}, bf16[2,512,256]{2,1,0:T(8,128)(2,1)}, u32[]{:S(2)}, u32[]{:S(2)}) collective-permute-start(bf16[2,512,256]{2,1,0:T(8,128)(2,1)} %get-tuple-element.41), channel_id=1, source_target_pairs={{0,72},{8,80},{16,88},{24,64},{32,104},{40,112},{48,120},{56,96},{... | collective-permute-start | bytes 1572872 | tf_op jit(solution)/shard_map/ppermute | solution.py:309
  76.2 63.4 %collective-permute-start.5 = (bf16[2,512,256]{2,1,0:T(8,128)(2,1)}, bf16[2,512,256]{2,1,0:T(8,128)(2,1)}, u32[]{:S(2)}, u32[]{:S(2)}) collective-permute-start(bf16[2,512,256]{2,1,0:T(8,128)(2,1)} %get-tuple-element.42), channel_id=1, source_target_pairs={{0,88},{8,64},{16,72},{24,80},{32,120},{40,96},{48,104},{56,112},{... | collective-permute-start | bytes 1572872 | tf_op jit(solution)/shard_map/ppermute | solution.py:309
  83.8 65.5 %collective-permute-start = (bf16[2,512,256]{2,1,0:T(8,128)(2,1)S(1)}, bf16[2,512,256]{2,1,0:T(8,128)(2,1)S(1)}, u32[]{:S(2)}, u32[]{:S(2)}) collective-permute-start(bf16[2,512,256]{2,1,0:T(8,128)(2,1)S(1)} %copy-done.29), channel_id=1, source_target_pairs={{0,16},{8,24},{16,0},{24,8},{32,48},{40,56},{48,32},{56,40},{64,80... | collective-permute-start | bytes 1572872 | tf_op jit(solution)/shard_map/ppermute | solution.py:309
  120.1 29.2 %collective-permute-start.1 = (bf16[2,512,256]{2,1,0:T(8,128)(2,1)S(1)}, bf16[2,512,256]{2,1,0:T(8,128)(2,1)S(1)}, u32[]{:S(2)}, u32[]{:S(2)}) collective-permute-start(bf16[2,512,256]{2,1,0:T(8,128)(2,1)S(1)} %copy-done.27), channel_id=1, source_target_pairs={{0,64},{8,72},{16,80},{24,88},{32,96},{40,104},{48,112},{56,120},{... | collective-permute-start | bytes 1572872 | tf_op jit(solution)/shard_map/ppermute | solution.py:309
  151.5 21.1 %collective-permute-start.15 = (bf16[256,512]{1,0:T(8,128)(2,1)S(1)}, bf16[256,512]{1,0:T(8,128)(2,1)S(1)}, u32[]{:S(2)}, u32[]{:S(2)}) collective-permute-start(bf16[256,512]{1,0:T(8,128)(2,1)S(1)} %get-tuple-element.61), channel_id=1, source_target_pairs={{0,4},{1,5},{2,6},{3,7},{4,0},{5,1},{6,2},{7,3},{8,12},{9,13},{10,... | collective-permute-start | bytes 786440 | tf_op jit(solution)/shard_map/ppermute | solution.py:314
  151.6 21.1 %collective-permute-start.16 = (bf16[256,512]{1,0:T(8,128)(2,1)S(1)}, bf16[256,512]{1,0:T(8,128)(2,1)S(1)}, u32[]{:S(2)}, u32[]{:S(2)}) collective-permute-start(bf16[256,512]{1,0:T(8,128)(2,1)S(1)} %get-tuple-element.62), channel_id=1, source_target_pairs={{0,5},{1,4},{2,7},{3,6},{4,1},{5,0},{6,3},{7,2},{8,13},{9,12},{10,... | collective-permute-start | bytes 786440 | tf_op jit(solution)/shard_map/ppermute | solution.py:314
  160.1 13.7 %collective-permute-start.17 = (bf16[256,512]{1,0:T(8,128)(2,1)S(1)}, bf16[256,512]{1,0:T(8,128)(2,1)S(1)}, u32[]{:S(2)}, u32[]{:S(2)}) collective-permute-start(bf16[256,512]{1,0:T(8,128)(2,1)S(1)} %get-tuple-element.63), channel_id=1, source_target_pairs={{0,2},{1,3},{2,4},{3,5},{4,6},{5,7},{6,0},{7,1},{8,10},{9,11},{10,... | collective-permute-start | bytes 786440 | tf_op jit(solution)/shard_map/ppermute | solution.py:314
  162.3 16.9 %collective-permute-start.18 = (bf16[256,512]{1,0:T(8,128)(2,1)S(1)}, bf16[256,512]{1,0:T(8,128)(2,1)S(1)}, u32[]{:S(2)}, u32[]{:S(2)}) collective-permute-start(bf16[256,512]{1,0:T(8,128)(2,1)S(1)} %get-tuple-element.64), channel_id=1, source_target_pairs={{0,3},{1,2},{2,5},{3,4},{4,7},{5,6},{6,1},{7,0},{8,11},{9,10},{10,... | collective-permute-start | bytes 786440 | tf_op jit(solution)/shard_map/ppermute | solution.py:314
  167.9 11.3 %collective-permute-start.19 = (bf16[256,512]{1,0:T(8,128)(2,1)S(1)}, bf16[256,512]{1,0:T(8,128)(2,1)S(1)}, u32[]{:S(2)}, u32[]{:S(2)}) collective-permute-start(bf16[256,512]{1,0:T(8,128)(2,1)S(1)} %get-tuple-element.65), channel_id=1, source_target_pairs={{0,6},{1,7},{2,0},{3,1},{4,2},{5,3},{6,4},{7,5},{8,14},{9,15},{10,... | collective-permute-start | bytes 786440 | tf_op jit(solution)/shard_map/ppermute | solution.py:314
  172.6 9.0 %collective-permute-start.20 = (bf16[256,512]{1,0:T(8,128)(2,1)S(1)}, bf16[256,512]{1,0:T(8,128)(2,1)S(1)}, u32[]{:S(2)}, u32[]{:S(2)}) collective-permute-start(bf16[256,512]{1,0:T(8,128)(2,1)S(1)} %get-tuple-element.66), channel_id=1, source_target_pairs={{0,7},{1,6},{2,1},{3,0},{4,3},{5,2},{6,5},{7,4},{8,15},{9,14},{10,... | collective-permute-start | bytes 786440 | tf_op jit(solution)/shard_map/ppermute | solution.py:314
  172.7 8.9 %collective-permute-start.21 = (bf16[256,512]{1,0:T(8,128)(2,1)S(1)}, bf16[256,512]{1,0:T(8,128)(2,1)S(1)}, u32[]{:S(2)}, u32[]{:S(2)}) collective-permute-start(bf16[256,512]{1,0:T(8,128)(2,1)S(1)} %get-tuple-element.68), channel_id=1, source_target_pairs={{0,1},{1,0},{2,3},{3,2},{4,5},{5,4},{6,7},{7,6},{8,9},{9,8},{10,11... | collective-permute-start | bytes 786440 | tf_op jit(solution)/shard_map/ppermute | solution.py:314
  (30 other events, 332.9 us)
